TPU v7x, 1024 devices: a whole 4x4x32 slice. The times are simulated.
1024 devices in a mesh: seq: 128 (over z, y), head: 8 (over x, core).
Axes of the slice: x: 4, y: 4, z: 32, core: 2. Of those that a mesh axis runs over, the one named last changes fastest.
Arguments:
- queries: bfloat16 [65536, 2048], P(('seq', 'head')), may hold values from -6 to 6
- output_gradient: bfloat16 [65536, 2048], P(('seq', 'head')), may hold values from -6 to 6
- outputs: bfloat16 [65536, 2048], P(('seq', 'head')), may hold values from -6 to 6
- key_vectors: bfloat16 [65536, 1024], P(('seq', 'head')), may hold values from -6 to 6
- values: bfloat16 [65536, 1024], P(('seq', 'head')), may hold values from -6 to 6
- logsum: float32 [16, 65536], P('head', 'seq'), as said below
- pair_list: int32 [500, 3], replicated, may hold values from 0 to 127, as said below
Outputs:
- grad_queries: bfloat16 [65536, 2048], P(('seq', 'head'))
- key_gradient: bfloat16 [65536, 1024], P(('seq', 'head'))
- value_gradient: bfloat16 [65536, 1024], P(('seq', 'head'))
Inputs may be any that keep to these rules, and one draw needn't show every extreme that they name: `pair_list`: every block b has the row (b, b, 1). Every other row (a, c, m) has 1 <= a - c <= 4 and m equal to 0 or 2. No pair appears twice; rows come in no particular order. A query block has between 1 and 5 rows, and block 127 has 5. `logsum`: each entry lies between ln(512) + 0.5 and ln(2560) + 0.5.
All inputs are finite; a program needn't handle non-finite values.
Results may differ from a plain program's by a relative error of at most 0.0054.
Values may be sent and summed in bfloat16 or wider, within the bound.
A program may use at most 32 MiB of HBM per device.

v0:
```python
import jax
import jax.numpy as jnp
from jax import lax
from jax.sharding import PartitionSpec as P

HEAD_SIZE = 128
KEY_VALUE_HEADS = 8
QUERY_HEADS = 16
WIN = 5


def from_behind(value, axis, steps):
    count = lax.axis_size(axis)
    first, last = (max(0, -steps), min(count, count - steps))
    return lax.ppermute(value, axis, [(source, source + steps) for source in range(first, last)])


def pair_grads(q_heads, do_heads, lse_heads, delta_heads, k_block, v_block, pair_code):
    score_scale = 1.0 / jnp.sqrt(jnp.float32(HEAD_SIZE))
    blk_rows = q_heads.shape[0]
    scores = (
        jnp.einsum("qkgd,skd->kgqs", q_heads, k_block, preferred_element_type=jnp.float32)
        * score_scale
    )
    row_ids = jnp.arange(blk_rows)[:, None]
    col_ids = jnp.arange(blk_rows)[None, :]
    allowed = (
        (pair_code == 1)
        | (pair_code == 2) & (col_ids <= row_ids)
        | (pair_code == 3) & (col_ids > row_ids)
    )
    probs = jnp.where(allowed, jnp.exp(scores - lse_heads[..., None]), jnp.float32(0.0))
    probs_low = probs.astype(jnp.bfloat16)
    grad_v = jnp.einsum("kgqs,qkgd->skd", probs_low, do_heads, preferred_element_type=jnp.float32)
    dprobs = jnp.einsum("qkgd,skd->kgqs", do_heads, v_block, preferred_element_type=jnp.float32)
    dscores = (probs * (dprobs - delta_heads[..., None]) * score_scale).astype(jnp.bfloat16)
    grad_q = jnp.einsum("kgqs,skd->qkgd", dscores, k_block, preferred_element_type=jnp.float32)
    grad_k = jnp.einsum("kgqs,qkgd->skd", dscores, q_heads, preferred_element_type=jnp.float32)
    return (grad_q, jnp.stack([grad_k, grad_v], axis=0))


def shards(queries, output_gradient, outputs, key_vectors, values, logsum, pair_list):
    number_of_heads = lax.axis_size("head")
    local_q = QUERY_HEADS // number_of_heads
    resident_key_value = KEY_VALUE_HEADS // number_of_heads
    group_count = QUERY_HEADS // KEY_VALUE_HEADS
    q_cols, do_cols, o_cols, k_cols, v_cols = (
        lax.all_to_all(queries, "head", split_axis=1, concat_axis=0, tiled=True),
        lax.all_to_all(output_gradient, "head", split_axis=1, concat_axis=0, tiled=True),
        lax.all_to_all(outputs, "head", split_axis=1, concat_axis=0, tiled=True),
        lax.all_to_all(key_vectors, "head", split_axis=1, concat_axis=0, tiled=True),
        lax.all_to_all(values, "head", split_axis=1, concat_axis=0, tiled=True),
    )
    blk_rows = q_cols.shape[0]
    delta_rows = jnp.sum(
        do_cols.astype(jnp.float32).reshape(blk_rows, local_q, HEAD_SIZE)
        * o_cols.astype(jnp.float32).reshape(blk_rows, local_q, HEAD_SIZE),
        axis=-1,
    )
    q_heads = q_cols.reshape(blk_rows, resident_key_value, group_count, HEAD_SIZE)
    do_heads = do_cols.reshape(blk_rows, resident_key_value, group_count, HEAD_SIZE)
    lse_heads = logsum.reshape(resident_key_value, group_count, blk_rows)
    delta_heads = delta_rows.T.reshape(resident_key_value, group_count, blk_rows)
    own_kv = jnp.stack(
        [
            k_cols.reshape(blk_rows, resident_key_value, HEAD_SIZE),
            v_cols.reshape(blk_rows, resident_key_value, HEAD_SIZE),
        ],
        axis=0,
    )
    my_block = lax.axis_index("seq")
    zero_q = jnp.zeros((blk_rows, resident_key_value, group_count, HEAD_SIZE), jnp.float32)
    zero_kv = jnp.zeros((2, blk_rows, resident_key_value, HEAD_SIZE), jnp.float32)
    acc_q = zero_q
    acc_kv = zero_kv
    for offset in range(WIN):
        if offset == 0:
            kv_block = own_kv
        else:
            kv_block = from_behind(own_kv, "seq", offset)
        matches = (pair_list[:, 0] == my_block) & (pair_list[:, 1] == my_block - offset)
        pair_code = jnp.sum(jnp.where(matches, pair_list[:, 2] + 1, 0))

        def compute_pair(operand):
            return pair_grads(
                q_heads, do_heads, lse_heads, delta_heads, operand[0], operand[1], pair_code
            )

        def skip_pair(operand):
            return (zero_q, zero_kv)

        part_q, part_kv = lax.cond(pair_code > 0, compute_pair, skip_pair, kv_block)
        acc_q = acc_q + part_q
        if offset == 0:
            acc_kv = part_kv
        else:
            acc_kv = acc_kv + from_behind(part_kv, "seq", -offset)
    grad_q_low = acc_q.reshape(blk_rows, local_q * HEAD_SIZE).astype(jnp.bfloat16)
    grad_k_low = acc_kv[0].reshape(blk_rows, resident_key_value * HEAD_SIZE).astype(jnp.bfloat16)
    grad_v_low = acc_kv[1].reshape(blk_rows, resident_key_value * HEAD_SIZE).astype(jnp.bfloat16)
    grad_queries, key_gradient, value_gradient = (
        lax.all_to_all(grad_q_low, "head", split_axis=0, concat_axis=1, tiled=True),
        lax.all_to_all(grad_k_low, "head", split_axis=0, concat_axis=1, tiled=True),
        lax.all_to_all(grad_v_low, "head", split_axis=0, concat_axis=1, tiled=True),
    )
    return (grad_queries, key_gradient, value_gradient)


def solution(mesh):
    in_specs = (
        P(("seq", "head"), None),
        P(("seq", "head"), None),
        P(("seq", "head"), None),
        P(("seq", "head"), None),
        P(("seq", "head"), None),
        P("head", "seq"),
        P(),
    )
    out_specs = (P(("seq", "head"), None), P(("seq", "head"), None), P(("seq", "head"), None))
    return jax.shard_map(shards, mesh=mesh, in_specs=in_specs, out_specs=out_specs, check_vma=False)
```

profile of v0, /device:TPU:736, one launch (start us, length us, event | category | flops | bytes accessed | tf_op | source)
XLA Modules:
  0.0 161.0 jit_solution(5767604781934633131)
XLA Ops:
  0.7 0.9 copy-done
  2.2 4.3 %all-to-all-start = ((bf16[64,8,128]{2,0,1:T(8,128)(2,1)}), bf16[64,8,128]{2,0,1:T(8,128)(2,1)S(1)}, u32[]{:S(2)}, u32[]{:S(2)}) async-start(bf16[64,8,128]{2,0,1:T(8,128)(2,1)} %copy_bitcast_fusion.6), calls=%async_computation | async-start | bytes 262144 | tf_op jit(solution)/shard_map/all_to_all | solution.py:51
  6.5 1.6 copy_bitcast_fusion.5
  8.1 4.5 %all-to-all-done = bf16[64,8,128]{2,0,1:T(8,128)(2,1)S(1)} async-done(((bf16[64,8,128]{2,0,1:T(8,128)(2,1)}), bf16[64,8,128]{2,0,1:T(8,128)(2,1)S(1)}, u32[]{:S(2)}, u32[]{:S(2)}) %all-to-all-start) | async-done | bytes 131104 | tf_op jit(solution)/shard_map/all_to_all | solution.py:51
  12.7 3.4 %all-to-all-start.2 = ((bf16[64,8,128]{2,0,1:T(8,128)(2,1)}), bf16[64,8,128]{2,0,1:T(8,128)(2,1)S(1)}, u32[]{:S(2)}, u32[]{:S(2)}) async-start(bf16[64,8,128]{2,0,1:T(8,128)(2,1)} %copy_bitcast_fusion.5), calls=%async_computation.2 | async-start | bytes 262144 | tf_op jit(solution)/shard_map/all_to_all | solution.py:52
  16.0 1.7 %copy.224 = bf16[8,8,8,256]{3,2,0,1:T(8,128)(2,1)} copy(bf16[8,8,8,256]{3,2,1,0:T(8,128)(2,1)} %bitcast.440) | data formatting | bytes 524288 | tf_op jit(solution)/shard_map/all_to_all | solution.py:48
  17.7 4.4 %all-to-all-done.2 = bf16[64,8,128]{2,0,1:T(8,128)(2,1)S(1)} async-done(((bf16[64,8,128]{2,0,1:T(8,128)(2,1)}), bf16[64,8,128]{2,0,1:T(8,128)(2,1)S(1)}, u32[]{:S(2)}, u32[]{:S(2)}) %all-to-all-start.2) | async-done | bytes 131104 | tf_op jit(solution)/shard_map/all_to_all | solution.py:52
  22.1 3.4 %all-to-all-start.1 = ((bf16[64,8,256]{2,0,1:T(8,128)(2,1)}), bf16[64,8,256]{2,0,1:T(8,128)(2,1)S(1)}, u32[]{:S(2)}, u32[]{:S(2)}) async-start(bf16[64,8,256]{2,0,1:T(8,128)(2,1)} %bitcast.424), calls=%async_computation.1 | async-start | bytes 524288 | tf_op jit(solution)/shard_map/all_to_all | solution.py:48
  25.5 0.7 copy.223
  26.2 6.7 %all-to-all-done.1 = bf16[64,8,256]{2,0,1:T(8,128)(2,1)S(1)} async-done(((bf16[64,8,256]{2,0,1:T(8,128)(2,1)}), bf16[64,8,256]{2,0,1:T(8,128)(2,1)S(1)}, u32[]{:S(2)}, u32[]{:S(2)}) %all-to-all-start.1) | async-done | bytes 262176 | tf_op jit(solution)/shard_map/all_to_all | solution.py:48
  33.0 3.4 %all-to-all-start.3 = ((bf16[64,8,256]{2,0,1:T(8,128)(2,1)}), bf16[64,8,256]{2,0,1:T(8,128)(2,1)S(1)}, u32[]{:S(2)}, u32[]{:S(2)}) async-start(bf16[64,8,256]{2,0,1:T(8,128)(2,1)} %bitcast.423), calls=%async_computation.3 | async-start | bytes 524288 | tf_op jit(solution)/shard_map/all_to_all | solution.py:49
  36.4 0.7 copy.222
  37.1 6.7 %all-to-all-done.3 = bf16[64,8,256]{2,0,1:T(8,128)(2,1)S(1)} async-done(((bf16[64,8,256]{2,0,1:T(8,128)(2,1)}), bf16[64,8,256]{2,0,1:T(8,128)(2,1)S(1)}, u32[]{:S(2)}, u32[]{:S(2)}) %all-to-all-start.3) | async-done | bytes 262176 | tf_op jit(solution)/shard_map/all_to_all | solution.py:49
  43.8 3.4 %all-to-all-start.4 = ((bf16[64,8,256]{2,0,1:T(8,128)(2,1)}), bf16[64,8,256]{2,0,1:T(8,128)(2,1)S(1)}, u32[]{:S(2)}, u32[]{:S(2)}) async-start(bf16[64,8,256]{2,0,1:T(8,128)(2,1)} %bitcast.422), calls=%async_computation.4 | async-start | bytes 524288 | tf_op jit(solution)/shard_map/all_to_all | solution.py:50
  47.3 2.9 %collective-permute-start.3 = (bf16[2,512,1,128]{3,1,2,0:T(8,128)(2,1)S(1)}, bf16[2,512,1,128]{3,1,2,0:T(8,128)(2,1)}, u32[]{:S(2)}, u32[]{:S(2)}) collective-permute-start(bf16[2,512,1,128]{3,1,2,0:T(8,128)(2,1)S(1)} %pad_maximum_fusion.5), channel_id=1, source_target_pairs={{0,32},{8,40},{16,48},{24,56},{32,64},{40,72},{48,80},{56,88},{64,... | collective-permute-start | bytes 786440 | tf_op jit(solution)/shard_map/ppermute | solution.py:15
  50.3 4.9 %collective-permute-start.2 = (bf16[2,512,1,128]{3,1,2,0:T(8,128)(2,1)S(1)}, bf16[2,512,1,128]{3,1,2,0:T(8,128)(2,1)S(1)}, u32[]{:S(2)}, u32[]{:S(2)}) collective-permute-start(bf16[2,512,1,128]{3,1,2,0:T(8,128)(2,1)S(1)} %pad_maximum_fusion.5), channel_id=1, source_target_pairs={{0,24},{8,32},{16,40},{24,48},{32,56},{40,64},{48,72},{56,80},{64,... | collective-permute-start | bytes 786440 | tf_op jit(solution)/shard_map/ppermute | solution.py:15
  55.2 3.0 %collective-permute-start.1 = (bf16[2,512,1,128]{3,1,2,0:T(8,128)(2,1)S(1)}, bf16[2,512,1,128]{3,1,2,0:T(8,128)(2,1)S(1)}, u32[]{:S(2)}, u32[]{:S(2)}) collective-permute-start(bf16[2,512,1,128]{3,1,2,0:T(8,128)(2,1)S(1)} %pad_maximum_fusion.5), channel_id=1, source_target_pairs={{0,16},{8,24},{16,32},{24,40},{32,48},{40,56},{48,64},{56,72},{64,... | collective-permute-start | bytes 786440 | tf_op jit(solution)/shard_map/ppermute | solution.py:15
  58.2 2.9 %collective-permute-start = (bf16[2,512,1,128]{3,1,2,0:T(8,128)(2,1)S(1)}, bf16[2,512,1,128]{3,1,2,0:T(8,128)(2,1)S(1)}, u32[]{:S(2)}, u32[]{:S(2)}) collective-permute-start(bf16[2,512,1,128]{3,1,2,0:T(8,128)(2,1)S(1)} %pad_maximum_fusion.5), channel_id=1, source_target_pairs={{0,8},{8,16},{16,24},{24,32},{32,40},{40,48},{48,56},{56,64},{64,7... | collective-permute-start | bytes 786440 | tf_op jit(solution)/shard_map/ppermute | solution.py:15
  61.1 0.8 fusion.125
  65.6 11.8 %collective-permute-done = bf16[2,512,1,128]{3,1,2,0:T(8,128)(2,1)S(1)} collective-permute-done((bf16[2,512,1,128]{3,1,2,0:T(8,128)(2,1)S(1)}, bf16[2,512,1,128]{3,1,2,0:T(8,128)(2,1)S(1)}, u32[]{:S(2)}, u32[]{:S(2)}) %collective-permute-start) | collective-permute-done | bytes 262176 | tf_op jit(solution)/shard_map/ppermute | solution.py:15
  77.4 5.5 %conditional.6 = (f32[512,1,2,128]{3,0,2,1:T(8,128)S(1)}, f32[2,512,1,128]{3,1,2,0:T(8,128)}) conditional(s32[]{:T(128)} %convert_element_type.79, () %tuple.50, (s32[]{:T(128)}, bf16[2,512,1,128]{3,1,2,0:T(8,128)(2,1)S(1)}, bf16[512,1,2,128]{3,2,0,1:T(2,128)(2,1)S(1)}, f32[2,512]{1,0:T(2,128)S(1)}, bf16[512,1,2,128]{3,2,0,1:T(2,128)(2,1)S(1)}, ...), branch_computations={%region_5.6_spmd, %region_6.7_spmd} | conditional | flops 676986880 | bytes 13516846 | solution.py:92
  79.6 0.7 fusion.24
  82.2 0.8 pad_maximum_fusion.1
  83.0 1.9 %collective-permute-start.4 = (f32[2,512,1,128]{3,1,2,0:T(8,128)}, f32[2,512,1,128]{3,1,2,0:T(8,128)}, u32[]{:S(2)}, u32[]{:S(2)}) collective-permute-start(f32[2,512,1,128]{3,1,2,0:T(8,128)} %get-tuple-element.114), channel_id=1, source_target_pairs={{8,0},{16,8},{24,16},{32,24},{40,32},{48,40},{56,48},{64,56},{72,6... | collective-permute-start | bytes 1572872 | tf_op jit(solution)/shard_map/ppermute | solution.py:15
  84.9 5.6 %conditional.7 = (f32[512,1,2,128]{3,0,2,1:T(8,128)S(1)}, f32[2,512,1,128]{3,1,2,0:T(8,128)}) conditional(s32[]{:T(128)} %convert_element_type.80, () %tuple.52, (s32[]{:T(128)}, bf16[2,512,1,128]{3,1,2,0:T(8,128)(2,1)S(1)}, bf16[512,1,2,128]{3,2,0,1:T(2,128)(2,1)S(1)}, f32[2,512]{1,0:T(2,128)S(1)}, bf16[512,1,2,128]{3,2,0,1:T(2,128)(2,1)S(1)}, ...), branch_computations={%region_8.9_spmd, %region_9.10_spmd} | conditional | flops 676986880 | bytes 13516846 | solution.py:92
  87.2 0.7 fusion.50
  89.7 0.8 pad_maximum_fusion.2
  90.5 1.9 %collective-permute-start.5 = (f32[2,512,1,128]{3,1,2,0:T(8,128)}, f32[2,512,1,128]{3,1,2,0:T(8,128)}, u32[]{:S(2)}, u32[]{:S(2)}) collective-permute-start(f32[2,512,1,128]{3,1,2,0:T(8,128)} %get-tuple-element.115), channel_id=1, source_target_pairs={{16,0},{24,8},{32,16},{40,24},{48,32},{56,40},{64,48},{72,56},{80,... | collective-permute-start | bytes 1572872 | tf_op jit(solution)/shard_map/ppermute | solution.py:15
  92.5 5.5 %conditional.8 = (f32[512,1,2,128]{3,0,2,1:T(8,128)S(1)}, f32[2,512,1,128]{3,1,2,0:T(8,128)}) conditional(s32[]{:T(128)} %convert_element_type.81, () %tuple.54, (s32[]{:T(128)}, bf16[2,512,1,128]{3,1,2,0:T(8,128)(2,1)S(1)}, bf16[512,1,2,128]{3,2,0,1:T(2,128)(2,1)S(1)}, f32[2,512]{1,0:T(2,128)S(1)}, bf16[512,1,2,128]{3,2,0,1:T(2,128)(2,1)S(1)}, ...), branch_computations={%region_11.12_spmd, %region_12.13_spmd} | conditional | flops 676986880 | bytes 13516846 | solution.py:92
  94.7 0.7 fusion.76
  97.2 0.8 pad_maximum_fusion.3
  98.0 1.9 %collective-permute-start.6 = (f32[2,512,1,128]{3,1,2,0:T(8,128)}, f32[2,512,1,128]{3,1,2,0:T(8,128)}, u32[]{:S(2)}, u32[]{:S(2)}) collective-permute-start(f32[2,512,1,128]{3,1,2,0:T(8,128)} %get-tuple-element.116), channel_id=1, source_target_pairs={{24,0},{32,8},{40,16},{48,24},{56,32},{64,40},{72,48},{80,56},{88,... | collective-permute-start | bytes 1572872 | tf_op jit(solution)/shard_map/ppermute | solution.py:15
  99.9 1.1 conditional.9
  99.9 0.8 broadcast_in_dim.76
  101.0 10.4 %collective-permute-start.7 = (f32[2,512,1,128]{3,1,2,0:T(8,128)}, f32[2,512,1,128]{3,1,2,0:T(8,128)}, u32[]{:S(2)}, u32[]{:S(2)}) collective-permute-start(f32[2,512,1,128]{3,1,2,0:T(8,128)} %get-tuple-element.117), channel_id=1, source_target_pairs={{32,0},{40,8},{48,16},{56,24},{64,32},{72,40},{80,48},{88,56},{96,... | collective-permute-start | bytes 1572872 | tf_op jit(solution)/shard_map/ppermute | solution.py:15
  111.9 4.5 %conditional.5 = (f32[512,1,2,128]{3,0,2,1:T(8,128)S(1)}, f32[2,512,1,128]{3,1,2,0:T(8,128)S(1)}) conditional(s32[]{:T(128)} %convert_element_type.75, () %tuple.48, (s32[]{:T(128)}, bf16[8,64,128]{2,1,0:T(8,128)(2,1)S(1)}, bf16[512,1,2,128]{3,2,0,1:T(2,128)(2,1)S(1)}, f32[2,512]{1,0:T(2,128)S(1)}, bf16[8,64,128]{2,1,0:T(8,128)(2,1)S(1)}, ...), branch_computations={%region_2.3_spmd, %region_3.4_spmd} | conditional | flops 676986880 | bytes 13516846 | solution.py:92
  113.9 0.7 fusion.4
  116.8 0.9 convert_element_type.84
  117.7 4.4 %all-to-all-start.5 = ((bf16[8,64,256]{2,1,0:T(8,128)(2,1)}), bf16[8,64,256]{2,1,0:T(8,128)(2,1)S(1)}, u32[]{:S(2)}, u32[]{:S(2)}) async-start(bf16[8,64,256]{2,1,0:T(8,128)(2,1)} %convert_element_type.84), calls=%async_computation.5 | async-start | bytes 524288 | tf_op jit(solution)/shard_map/all_to_all | solution.py:102
  122.2 2.0 %collective-permute-done.6 = f32[2,512,1,128]{3,1,2,0:T(8,128)} collective-permute-done((f32[2,512,1,128]{3,1,2,0:T(8,128)}, f32[2,512,1,128]{3,1,2,0:T(8,128)}, u32[]{:S(2)}, u32[]{:S(2)}) %collective-permute-start.6) | collective-permute-done | bytes 524320 | tf_op jit(solution)/shard_map/ppermute | solution.py:15
  124.2 14.9 %collective-permute-done.7 = f32[2,512,1,128]{3,1,2,0:T(8,128)} collective-permute-done((f32[2,512,1,128]{3,1,2,0:T(8,128)}, f32[2,512,1,128]{3,1,2,0:T(8,128)}, u32[]{:S(2)}, u32[]{:S(2)}) %collective-permute-start.7) | collective-permute-done | bytes 524320 | tf_op jit(solution)/shard_map/ppermute | solution.py:15
  139.1 1.6 %add_convert_fusion = bf16[2,512,1,128]{3,1,2,0:T(8,128)(2,1)S(1)} fusion(f32[2,512,1,128]{3,1,2,0:T(8,128)} %collective-permute-done.7, f32[2,512,1,128]{3,1,2,0:T(8,128)} %collective-permute-done.6, f32[2,512,1,128]{3,1,2,0:T(8,128)} %collective-permute-done.5, f32[2,512,1,128]{3,1,2,0:T(8,128)S(1)} %get-tuple-element.113, ...), kind=kLoop, calls=%fused_computation.165 | loop fusion | flops 655360 | bytes 2883584 | tf_op jit(solution)/shard_map/convert.2
  140.7 0.7 fusion.129
  141.5 3.4 %all-to-all-start.6 = ((bf16[8,64,128]{2,1,0:T(8,128)(2,1)}), bf16[8,64,128]{2,1,0:T(8,128)(2,1)S(1)}, u32[]{:S(2)}, u32[]{:S(2)}) async-start(bf16[8,64,128]{2,1,0:T(8,128)(2,1)} %bitcast.134), calls=%async_computation.6 | async-start | bytes 262144 | tf_op jit(solution)/shard_map/all_to_all | solution.py:103
  144.8 0.7 copy.132
  145.6 5.3 %all-to-all-done.6 = bf16[8,64,128]{2,1,0:T(8,128)(2,1)S(1)} async-done(((bf16[8,64,128]{2,1,0:T(8,128)(2,1)}), bf16[8,64,128]{2,1,0:T(8,128)(2,1)S(1)}, u32[]{:S(2)}, u32[]{:S(2)}) %all-to-all-start.6) | async-done | bytes 131104 | tf_op jit(solution)/shard_map/all_to_all | solution.py:103
  150.9 3.4 %all-to-all-start.7 = ((bf16[8,64,128]{2,1,0:T(8,128)(2,1)}), bf16[8,64,128]{2,1,0:T(8,128)(2,1)S(1)}, u32[]{:S(2)}, u32[]{:S(2)}) async-start(bf16[8,64,128]{2,1,0:T(8,128)(2,1)} %bitcast.136), calls=%async_computation.7 | async-start | bytes 262144 | tf_op jit(solution)/shard_map/all_to_all | solution.py:104
  155.0 5.4 %all-to-all-done.7 = bf16[8,64,128]{2,1,0:T(8,128)(2,1)S(1)} async-done(((bf16[8,64,128]{2,1,0:T(8,128)(2,1)}), bf16[8,64,128]{2,1,0:T(8,128)(2,1)S(1)}, u32[]{:S(2)}, u32[]{:S(2)}) %all-to-all-start.7) | async-done | bytes 131104 | tf_op jit(solution)/shard_map/all_to_all | solution.py:104
  (53 shorter events, 11.8 us)
Async XLA Ops:
  0.6 0.9 copy-start
  0.6 24.9 %copy-start.1 = (bf16[64,2048]{1,0:T(8,128)(2,1)S(1)}, bf16[64,2048]{1,0:T(8,128)(2,1)}, u32[]{:S(2)}) copy-start(bf16[64,2048]{1,0:T(8,128)(2,1)} %param.18) | copy-start | bytes 786436
  0.7 35.7 %copy-start.2 = (bf16[64,2048]{1,0:T(8,128)(2,1)S(1)}, bf16[64,2048]{1,0:T(8,128)(2,1)}, u32[]{:S(2)}) copy-start(bf16[64,2048]{1,0:T(8,128)(2,1)} %param.19) | copy-start | bytes 786436
  2.2 10.4 %all-to-all-start = ((bf16[64,8,128]{2,0,1:T(8,128)(2,1)}), bf16[64,8,128]{2,0,1:T(8,128)(2,1)S(1)}, u32[]{:S(2)}, u32[]{:S(2)}) async-start(bf16[64,8,128]{2,0,1:T(8,128)(2,1)} %copy_bitcast_fusion.6), calls=%async_computation | async-start | bytes 262144 | tf_op jit(solution)/shard_map/all_to_all | solution.py:51
  6.5 54.6 %copy-start.3 = (s32[500,3]{0,1:T(4,128)S(1)}, s32[500,3]{0,1:T(4,128)}, u32[]{:S(2)}) copy-start(s32[500,3]{0,1:T(4,128)} %param.23) | copy-start | bytes 18004
  12.7 9.4 %all-to-all-start.2 = ((bf16[64,8,128]{2,0,1:T(8,128)(2,1)}), bf16[64,8,128]{2,0,1:T(8,128)(2,1)S(1)}, u32[]{:S(2)}, u32[]{:S(2)}) async-start(bf16[64,8,128]{2,0,1:T(8,128)(2,1)} %copy_bitcast_fusion.5), calls=%async_computation.2 | async-start | bytes 262144 | tf_op jit(solution)/shard_map/all_to_all | solution.py:52
  22.1 10.9 %all-to-all-start.1 = ((bf16[64,8,256]{2,0,1:T(8,128)(2,1)}), bf16[64,8,256]{2,0,1:T(8,128)(2,1)S(1)}, u32[]{:S(2)}, u32[]{:S(2)}) async-start(bf16[64,8,256]{2,0,1:T(8,128)(2,1)} %bitcast.424), calls=%async_computation.1 | async-start | bytes 524288 | tf_op jit(solution)/shard_map/all_to_all | solution.py:48
  33.0 10.9 %all-to-all-start.3 = ((bf16[64,8,256]{2,0,1:T(8,128)(2,1)}), bf16[64,8,256]{2,0,1:T(8,128)(2,1)S(1)}, u32[]{:S(2)}, u32[]{:S(2)}) async-start(bf16[64,8,256]{2,0,1:T(8,128)(2,1)} %bitcast.423), calls=%async_computation.3 | async-start | bytes 524288 | tf_op jit(solution)/shard_map/all_to_all | solution.py:49
  43.8 20.8 %all-to-all-start.4 = ((bf16[64,8,256]{2,0,1:T(8,128)(2,1)}), bf16[64,8,256]{2,0,1:T(8,128)(2,1)S(1)}, u32[]{:S(2)}, u32[]{:S(2)}) async-start(bf16[64,8,256]{2,0,1:T(8,128)(2,1)} %bitcast.422), calls=%async_computation.4 | async-start | bytes 524288 | tf_op jit(solution)/shard_map/all_to_all | solution.py:50
  47.3 30.1 %copy-start.4 = (f32[2,512]{1,0:T(2,128)S(1)}, f32[2,512]{1,0:T(2,128)}, u32[]{:S(2)}) copy-start(f32[2,512]{1,0:T(2,128)} %param.22) | copy-start | bytes 12292
  47.3 52.6 %collective-permute-start.3 = (bf16[2,512,1,128]{3,1,2,0:T(8,128)(2,1)S(1)}, bf16[2,512,1,128]{3,1,2,0:T(8,128)(2,1)}, u32[]{:S(2)}, u32[]{:S(2)}) collective-permute-start(bf16[2,512,1,128]{3,1,2,0:T(8,128)(2,1)S(1)} %pad_maximum_fusion.5), channel_id=1, source_target_pairs={{0,32},{8,40},{16,48},{24,56},{32,64},{40,72},{48,80},{56,88},{64,... | collective-permute-start | bytes 786440 | tf_op jit(solution)/shard_map/ppermute | solution.py:15
  50.3 42.2 %collective-permute-start.2 = (bf16[2,512,1,128]{3,1,2,0:T(8,128)(2,1)S(1)}, bf16[2,512,1,128]{3,1,2,0:T(8,128)(2,1)S(1)}, u32[]{:S(2)}, u32[]{:S(2)}) collective-permute-start(bf16[2,512,1,128]{3,1,2,0:T(8,128)(2,1)S(1)} %pad_maximum_fusion.5), channel_id=1, source_target_pairs={{0,24},{8,32},{16,40},{24,48},{32,56},{40,64},{48,72},{56,80},{64,... | collective-permute-start | bytes 786440 | tf_op jit(solution)/shard_map/ppermute | solution.py:15
  55.2 29.7 %collective-permute-start.1 = (bf16[2,512,1,128]{3,1,2,0:T(8,128)(2,1)S(1)}, bf16[2,512,1,128]{3,1,2,0:T(8,128)(2,1)S(1)}, u32[]{:S(2)}, u32[]{:S(2)}) collective-permute-start(bf16[2,512,1,128]{3,1,2,0:T(8,128)(2,1)S(1)} %pad_maximum_fusion.5), channel_id=1, source_target_pairs={{0,16},{8,24},{16,32},{24,40},{32,48},{40,56},{48,64},{56,72},{64,... | collective-permute-start | bytes 786440 | tf_op jit(solution)/shard_map/ppermute | solution.py:15
  58.2 19.3 %collective-permute-start = (bf16[2,512,1,128]{3,1,2,0:T(8,128)(2,1)S(1)}, bf16[2,512,1,128]{3,1,2,0:T(8,128)(2,1)S(1)}, u32[]{:S(2)}, u32[]{:S(2)}) collective-permute-start(bf16[2,512,1,128]{3,1,2,0:T(8,128)(2,1)S(1)} %pad_maximum_fusion.5), channel_id=1, source_target_pairs={{0,8},{8,16},{16,24},{24,32},{32,40},{40,48},{48,56},{56,64},{64,7... | collective-permute-start | bytes 786440 | tf_op jit(solution)/shard_map/ppermute | solution.py:15
  83.0 39.2 %collective-permute-start.4 = (f32[2,512,1,128]{3,1,2,0:T(8,128)}, f32[2,512,1,128]{3,1,2,0:T(8,128)}, u32[]{:S(2)}, u32[]{:S(2)}) collective-permute-start(f32[2,512,1,128]{3,1,2,0:T(8,128)} %get-tuple-element.114), channel_id=1, source_target_pairs={{8,0},{16,8},{24,16},{32,24},{40,32},{48,40},{56,48},{64,56},{72,6... | collective-permute-start | bytes 1572872 | tf_op jit(solution)/shard_map/ppermute | solution.py:15
  90.5 31.6 %collective-permute-start.5 = (f32[2,512,1,128]{3,1,2,0:T(8,128)}, f32[2,512,1,128]{3,1,2,0:T(8,128)}, u32[]{:S(2)}, u32[]{:S(2)}) collective-permute-start(f32[2,512,1,128]{3,1,2,0:T(8,128)} %get-tuple-element.115), channel_id=1, source_target_pairs={{16,0},{24,8},{32,16},{40,24},{48,32},{56,40},{64,48},{72,56},{80,... | collective-permute-start | bytes 1572872 | tf_op jit(solution)/shard_map/ppermute | solution.py:15
  98.0 26.2 %collective-permute-start.6 = (f32[2,512,1,128]{3,1,2,0:T(8,128)}, f32[2,512,1,128]{3,1,2,0:T(8,128)}, u32[]{:S(2)}, u32[]{:S(2)}) collective-permute-start(f32[2,512,1,128]{3,1,2,0:T(8,128)} %get-tuple-element.116), channel_id=1, source_target_pairs={{24,0},{32,8},{40,16},{48,24},{56,32},{64,40},{72,48},{80,56},{88,... | collective-permute-start | bytes 1572872 | tf_op jit(solution)/shard_map/ppermute | solution.py:15
  101.0 38.1 %collective-permute-start.7 = (f32[2,512,1,128]{3,1,2,0:T(8,128)}, f32[2,512,1,128]{3,1,2,0:T(8,128)}, u32[]{:S(2)}, u32[]{:S(2)}) collective-permute-start(f32[2,512,1,128]{3,1,2,0:T(8,128)} %get-tuple-element.117), channel_id=1, source_target_pairs={{32,0},{40,8},{48,16},{56,24},{64,32},{72,40},{80,48},{88,56},{96,... | collective-permute-start | bytes 1572872 | tf_op jit(solution)/shard_map/ppermute | solution.py:15
  117.7 23.7 %all-to-all-start.5 = ((bf16[8,64,256]{2,1,0:T(8,128)(2,1)}), bf16[8,64,256]{2,1,0:T(8,128)(2,1)S(1)}, u32[]{:S(2)}, u32[]{:S(2)}) async-start(bf16[8,64,256]{2,1,0:T(8,128)(2,1)} %convert_element_type.84), calls=%async_computation.5 | async-start | bytes 524288 | tf_op jit(solution)/shard_map/all_to_all | solution.py:102
  141.5 9.4 %all-to-all-start.6 = ((bf16[8,64,128]{2,1,0:T(8,128)(2,1)}), bf16[8,64,128]{2,1,0:T(8,128)(2,1)S(1)}, u32[]{:S(2)}, u32[]{:S(2)}) async-start(bf16[8,64,128]{2,1,0:T(8,128)(2,1)} %bitcast.134), calls=%async_computation.6 | async-start | bytes 262144 | tf_op jit(solution)/shard_map/all_to_all | solution.py:103
  150.9 9.4 %all-to-all-start.7 = ((bf16[8,64,128]{2,1,0:T(8,128)(2,1)}), bf16[8,64,128]{2,1,0:T(8,128)(2,1)S(1)}, u32[]{:S(2)}, u32[]{:S(2)}) async-start(bf16[8,64,128]{2,1,0:T(8,128)(2,1)} %bitcast.136), calls=%async_computation.7 | async-start | bytes 262144 | tf_op jit(solution)/shard_map/all_to_all | solution.py:104
where the time goes:
time: 162 us; the launch traced here: 161 us
  waiting for transfers between devices  61.9 us (38%)
  starting transfers between devices  58.9 us (36%)
  local copies, waits for them, and re-layouts  11.9 us (7%)
  matrix products  9.89 us (6%)
  loops' own time  8 us (5%)
  other arithmetic  6.28 us (4%)
  between operations  4.15 us (3%)
    ppermute x8, starting transfers between devices, from_behind(): lax.ppermute(value, axis, [(source, source + steps) for source in range(f...  29.8 us
    ppermute x8, waiting for transfers between devices, from_behind(): lax.ppermute(value, axis, [(source, source + steps) for source in range(f...  28.8 us
    another operation x5, loops' own time, shards(): part_q, part_kv = lax.cond(pair_code > 0, compute_pair, skip_pair, kv_block)  8 us
    all_to_all x1, waiting for transfers between devices, shards(): lax.all_to_all(queries, 'head', split_axis=1, concat_axis=0, tiled=True)  6.73 us
    all_to_all x1, waiting for transfers between devices, shards(): lax.all_to_all(output_gradient, 'head', split_axis=1, concat_axis=0, tile...  6.72 us
    all_to_all x1, waiting for transfers between devices, shards(): lax.all_to_all(grad_v_low, 'head', split_axis=0, concat_axis=1, tiled=True)  5.38 us
    all_to_all x1, waiting for transfers between devices, shards(): lax.all_to_all(grad_k_low, 'head', split_axis=0, concat_axis=1, tiled=True)  5.33 us
    all_to_all x1, waiting for transfers between devices, shards(): lax.all_to_all(key_vectors, 'head', split_axis=1, concat_axis=0, tiled=True)  4.54 us
  transfers between devices with their start and end apart: 16, of which 9 were waited for; matrix products, arithmetic and copies ran while one was open for 16% of the time, Pallas kernels for 0%

commit v1 on v0

v1 whole, which is shorter than its diff:
```python
import jax
import jax.numpy as jnp
from jax import lax
from jax.experimental import pallas as pl
from jax.experimental.pallas import tpu as pltpu
from jax.sharding import PartitionSpec as P

D = 128
BLK = 512
TOK = 64
HEADS = 8
SEQ = 128
WIN = 5
LOG2E = 1.4426950408889634
SCALE = 1.0 / D**0.5
BIG = 1e30
F32 = jnp.float32
BF16 = jnp.bfloat16
MESH = pl.DeviceIdType.MESH
PEER_ORDER = (4, 3, 5, 2, 6, 1, 7)


def dot_nt(a, b):
    return lax.dot_general(a, b, (((1,), (1,)), ((), ())), preferred_element_type=F32)


def dot_nn(a, b):
    return lax.dot_general(a, b, (((1,), (0,)), ((), ())), preferred_element_type=F32)


def wait_bytes(ref, sem):
    pltpu.make_async_copy(ref, ref, sem).wait()


def kernel(
    q_hbm, do_hbm, o_hbm, k_hbm, v_hbm, lse_hbm, pairs_hbm,
    oq_ref, ok_ref, ov_ref,
    kv, qs, dos, do_own, o_own, lse, pairs, dls, dlr, accq, own_g, gsend, grecv, fin_q, fin_kv,
    loc_sem, in_recv, in_send, kv_recv, kv_send, g_recv, g_send, out_recv, out_send,
):
    s = lax.axis_index("seq")
    h = lax.axis_index("head")

    c_do = pltpu.make_async_copy(do_hbm, do_own, loc_sem.at[0])
    c_o = pltpu.make_async_copy(o_hbm, o_own, loc_sem.at[1])
    c_lse = pltpu.make_async_copy(lse_hbm, lse, loc_sem.at[2])
    c_pairs = pltpu.make_async_copy(pairs_hbm, pairs, loc_sem.at[3])
    for c in (c_do, c_o, c_lse, c_pairs):
        c.start()

    barrier = pltpu.get_barrier_semaphore()
    for j in range(1, HEADS):
        pl.semaphore_signal(barrier, inc=1, device_id=(s, lax.rem(h + j, HEADS)), device_id_type=MESH)
    for j in range(1, WIN):
        pl.semaphore_signal(barrier, inc=1, device_id=(lax.rem(s + j, SEQ), h), device_id_type=MESH)
        pl.semaphore_signal(
            barrier, inc=1, device_id=(lax.rem(s + SEQ - j, SEQ), h), device_id_type=MESH
        )
    pl.semaphore_wait(barrier, HEADS - 1 + 2 * (WIN - 1))

    my_rows = pl.ds(pl.multiple_of(h * TOK, TOK), TOK)

    def cols(p, width):
        return pl.ds(pl.multiple_of(p * width, width), width)

    def spread(src, dst, width, n):
        for j in PEER_ORDER:
            p = lax.rem(h + j, HEADS)
            pltpu.make_async_remote_copy(
                src_ref=src.at[:, cols(p, width)],
                dst_ref=dst,
                send_sem=in_send.at[n],
                recv_sem=in_recv.at[0 if n < 2 else n - 1],
                device_id=(s, p),
                device_id_type=MESH,
            ).start()
        pltpu.make_async_copy(
            src.at[:, cols(h, width)], dst, in_recv.at[0 if n < 2 else n - 1]
        ).start()

    spread(k_hbm, kv.at[0, my_rows, 0:D], D, 0)
    spread(v_hbm, kv.at[0, my_rows, D : 2 * D], D, 1)
    spread(q_hbm, qs.at[my_rows, :], 2 * D, 2)
    spread(do_hbm, dos.at[my_rows, :], 2 * D, 3)

    c_do.wait()
    c_o.wait()
    row8 = lax.broadcasted_iota(jnp.int32, (8, 2 * D), 0)
    col8 = lax.broadcasted_iota(jnp.int32, (8, 2 * D), 1)
    select = jnp.where((col8 >= row8 * D) & (col8 < row8 * D + D), 1.0, 0.0).astype(BF16)
    lane = lax.broadcasted_iota(jnp.int32, (8, D), 1)
    low = lax.rem(h, 2) * TOK
    mine = jnp.where((lane >= low) & (lane < low + TOK), 1.0, 0.0)
    for p in range(HEADS):
        c = slice(p * 2 * D, (p + 1) * 2 * D)
        prod = do_own[:, c].astype(F32) * o_own[:, c].astype(F32)
        prod = jnp.concatenate([prod, prod], axis=0)
        hi = prod.astype(BF16)
        mid = (prod - hi.astype(F32)).astype(BF16)
        dls[p] = (dot_nt(select, hi) + dot_nt(select, mid)) * mine
    for j in PEER_ORDER:
        p = lax.rem(h + j, HEADS)
        pltpu.make_async_remote_copy(
            src_ref=dls.at[p],
            dst_ref=dlr.at[h],
            send_sem=in_send.at[4],
            recv_sem=in_recv.at[3],
            device_id=(s, p),
            device_id_type=MESH,
        ).start()
    pltpu.make_async_copy(dls.at[h], dlr.at[h], in_recv.at[3]).start()

    wait_bytes(kv.at[0], in_recv.at[0])
    for d in (2, 4, 3, 1):
        pltpu.make_async_remote_copy(
            src_ref=kv.at[0],
            dst_ref=kv.at[d],
            send_sem=kv_send,
            recv_sem=kv_recv.at[d],
            device_id=(lax.rem(s + d, SEQ), h),
            device_id_type=MESH,
        ).start()

    c_lse.wait()
    c_pairs.wait()
    pa = pairs[0:1, :]
    pc = pairs[1:2, :]
    pm = pairs[2:3, :]
    accq[...] = jnp.zeros_like(accq)

    wait_bytes(qs, in_recv.at[1])
    wait_bytes(dos, in_recv.at[2])
    wait_bytes(dlr, in_recv.at[3])
    delta = jnp.concatenate([dlr[2 * i] + dlr[2 * i + 1] for i in range(HEADS // 2)], axis=1)
    lse2 = lse[...] * LOG2E

    def pair_step(pd, carry):
        d = lax.rem(3 * pd, WIN)

        @pl.when(pd > 0)
        def _():
            wait_bytes(kv.at[d], kv_recv.at[d])

        match = (pa == s) & (pc == s - d)
        code = jnp.max(jnp.where(match, pm + 1, 0), axis=1, keepdims=True)
        lo = jnp.where((code == 1) | (code == 2), -BLK, jnp.where(code == 3, 0, BLK))
        hi = jnp.where(code == 2, 1, BLK)
        diff = lax.broadcasted_iota(jnp.int32, (BLK, BLK), 0) - lax.broadcasted_iota(
            jnp.int32, (BLK, BLK), 1
        )
        bias = jnp.where((diff > lo) & (diff < hi), 0.0, BIG).astype(F32)
        k = kv[d, :, 0:D]
        v = kv[d, :, D : 2 * D]
        kt = k.T
        gk = jnp.zeros((BLK, D), F32)
        gv = jnp.zeros((BLK, D), F32)
        for g in range(2):
            c = slice(g * D, (g + 1) * D)
            q = qs[:, c]
            do = dos[:, c]
            prob = jnp.exp2(dot_nt(k, q) * (SCALE * LOG2E) - lse2[g : g + 1, :] - bias)
            ds = (prob * (dot_nt(v, do) - delta[g : g + 1, :])).astype(BF16)
            gv = gv + dot_nn(prob.astype(BF16), do)
            gk = gk + dot_nn(ds, q)
            accq[c, :] += dot_nn(kt, ds)

        @pl.when(pd == 0)
        def _():
            own_g[:, 0:D] = gk
            own_g[:, D : 2 * D] = gv

        @pl.when(pd > 0)
        def _():
            gsend[d, :, 0:D] = gk.astype(BF16)
            gsend[d, :, D : 2 * D] = gv.astype(BF16)
            pltpu.make_async_remote_copy(
                src_ref=gsend.at[d],
                dst_ref=grecv.at[d],
                send_sem=g_send,
                recv_sem=g_recv.at[d],
                device_id=(lax.rem(s + SEQ - d, SEQ), h),
                device_id_type=MESH,
            ).start()

        return carry

    lax.fori_loop(0, WIN, pair_step, 0)

    def gather(src, col, width, dst, n):
        for j in PEER_ORDER:
            p = lax.rem(h + j, HEADS)
            pltpu.make_async_remote_copy(
                src_ref=src.at[cols(p, TOK), col],
                dst_ref=dst.at[:, cols(h, width)],
                send_sem=out_send.at[n],
                recv_sem=out_recv.at[n],
                device_id=(s, p),
                device_id_type=MESH,
            ).start()
        pltpu.make_async_copy(
            src.at[my_rows, col], dst.at[:, cols(h, width)], out_recv.at[n]
        ).start()

    for g in range(2):
        c = slice(g * D, (g + 1) * D)
        fin_q[:, c] = (accq[c, :] * SCALE).T.astype(BF16)
    gather(fin_q, slice(0, 2 * D), 2 * D, oq_ref, 0)

    for d in range(1, WIN):
        wait_bytes(grecv.at[d], g_recv.at[d])
    tot = own_g[...]
    for d in range(1, WIN):
        tot = tot + grecv[d].astype(F32)
    fin_kv[:, 0:D] = (tot[:, 0:D] * SCALE).astype(BF16)
    fin_kv[:, D : 2 * D] = tot[:, D : 2 * D].astype(BF16)
    gather(fin_kv, slice(0, D), D, ok_ref, 1)
    gather(fin_kv, slice(D, 2 * D), D, ov_ref, 2)

    most = (HEADS - 1) * TOK
    wait_bytes(kv.at[0, 0:most, 0:D], in_send.at[0])
    wait_bytes(kv.at[0, 0:most, 0:D], in_send.at[1])
    wait_bytes(qs.at[0:most], in_send.at[2])
    wait_bytes(qs.at[0:most], in_send.at[3])
    wait_bytes(dlr.at[0 : HEADS - 1], in_send.at[4])
    wait_bytes(kv.at[1:WIN], kv_send)
    wait_bytes(gsend.at[1:WIN], g_send)
    wait_bytes(fin_q.at[0:most], out_send.at[0])
    wait_bytes(fin_kv.at[0:most, 0:D], out_send.at[1])
    wait_bytes(fin_kv.at[0:most, 0:D], out_send.at[2])
    wait_bytes(oq_ref, out_recv.at[0])
    wait_bytes(ok_ref, out_recv.at[1])
    wait_bytes(ov_ref, out_recv.at[2])


def shards(queries, output_gradient, outputs, key_vectors, values, logsum, pair_list):
    any_spec = pl.BlockSpec(memory_space=pl.ANY)
    return pl.pallas_call(
        kernel,
        out_shape=(
            jax.ShapeDtypeStruct((TOK, 2 * D * HEADS), BF16),
            jax.ShapeDtypeStruct((TOK, D * HEADS), BF16),
            jax.ShapeDtypeStruct((TOK, D * HEADS), BF16),
        ),
        in_specs=[any_spec] * 7,
        out_specs=(any_spec,) * 3,
        scratch_shapes=[
            pltpu.VMEM((WIN, BLK, 2 * D), BF16),
            pltpu.VMEM((BLK, 2 * D), BF16),
            pltpu.VMEM((BLK, 2 * D), BF16),
            pltpu.VMEM((TOK, 2 * D * HEADS), BF16),
            pltpu.VMEM((TOK, 2 * D * HEADS), BF16),
            pltpu.VMEM((2, BLK), F32),
            pltpu.VMEM((3, 500), jnp.int32),
            pltpu.VMEM((HEADS, 8, D), F32),
            pltpu.VMEM((HEADS, 8, D), F32),
            pltpu.VMEM((2 * D, BLK), F32),
            pltpu.VMEM((BLK, 2 * D), F32),
            pltpu.VMEM((WIN, BLK, 2 * D), BF16),
            pltpu.VMEM((WIN, BLK, 2 * D), BF16),
            pltpu.VMEM((BLK, 2 * D), BF16),
            pltpu.VMEM((BLK, 2 * D), BF16),
            pltpu.SemaphoreType.DMA((4,)),
            pltpu.SemaphoreType.DMA((4,)),
            pltpu.SemaphoreType.DMA((5,)),
            pltpu.SemaphoreType.DMA((WIN,)),
            pltpu.SemaphoreType.DMA,
            pltpu.SemaphoreType.DMA((WIN,)),
            pltpu.SemaphoreType.DMA,
            pltpu.SemaphoreType.DMA((3,)),
            pltpu.SemaphoreType.DMA((3,)),
        ],
        compiler_params=pltpu.CompilerParams(
            collective_id=0, has_side_effects=True, vmem_limit_bytes=60 * 2**20
        ),
        cost_estimate=pl.CostEstimate(
            flops=2 * WIN * 2 * 5 * BLK * BLK * D,
            bytes_accessed=3 * 2**19,
            transcendentals=WIN * 2 * BLK * BLK,
        ),
    )(
        queries, output_gradient, outputs, key_vectors, values, logsum, jnp.transpose(pair_list)
    )


def solution(mesh):
    tok = P(("seq", "head"), None)
    return jax.shard_map(
        shards,
        mesh=mesh,
        in_specs=(tok, tok, tok, tok, tok, P("head", "seq"), P()),
        out_specs=(tok, tok, tok),
        check_vma=False,
    )
```

time: 162 us -> 81 us (0.50)
  the two profiles are of different devices: /device:TPU:736 before, /device:TPU:17 now
where the time goes in v1:
time: 81 us; the launch traced here: 80.8 us
  Pallas kernels  76.8 us (95%)
  local copies, waits for them, and re-layouts  3.31 us (4%)
    pallas_call x1, Pallas kernels, shards(): pl.pallas_call(kernel, out_shape=(jax.ShapeDtypeStruct((TOK, 2 * D * HEAD...  76.8 us
    unnamed x7, local copies, waits for them, and re-layouts  3.31 us

profile of v1, /device:TPU:17, one launch (start us, length us, event | category | flops | bytes accessed | tf_op | source)
XLA Modules:
  0.0 80.8 jit_solution(7868798844201036604)
XLA Ops:
  0.6 76.8 %shard_map.94 = (bf16[64,2048]{1,0:T(8,128)(2,1)}, bf16[64,1024]{1,0:T(8,128)(2,1)}, bf16[64,1024]{1,0:T(8,128)(2,1)}) custom-call(bf16[64,2048]{1,0:T(8,128)(2,1)} %q_hbm.1, bf16[64,2048]{1,0:T(8,128)(2,1)} %do_hbm.1, bf16[64,2048]{1,0:T(8,128)(2,1)} %o_hbm.1, bf16[64,1024]{1,0:T(8,128)(2,1)} %k_hbm.1, bf16[64,1024]{1,0:T(8,128)(2,1)} %v_hbm.1, ...), custom_call_target="tpu_custom_call" | custom-call | flops 3355443200 | bytes 1572864 | tf_op jit(solution)/shard_map/pallas_call | solution.py:237
  77.4 0.0 copy-start.1
  77.4 1.7 %copy.13 = bf16[64,2048]{1,0:T(8,128)(2,1)} copy(bf16[64,2048]{1,0:T(8,128)(2,1)} %get-tuple-element.6) | data formatting | bytes 524288
  79.1 0.0 copy-done.1
  79.1 0.0 copy-start
  79.2 0.7 copy.14
  79.8 0.3 copy-done
  80.1 0.7 copy.15
Async XLA Ops:
  77.4 1.7 %copy-start.1 = (bf16[64,1024]{1,0:T(8,128)(2,1)S(1)}, bf16[64,1024]{1,0:T(8,128)(2,1)}, u32[]{:S(2)}) copy-start(bf16[64,1024]{1,0:T(8,128)(2,1)} %get-tuple-element.7) | copy-start | bytes 393220
  79.1 1.0 %copy-start = (bf16[64,1024]{1,0:T(8,128)(2,1)S(1)}, bf16[64,1024]{1,0:T(8,128)(2,1)}, u32[]{:S(2)}) copy-start(bf16[64,1024]{1,0:T(8,128)(2,1)} %get-tuple-element.8) | copy-start | bytes 393220

commit v2 on v1

--- a/solution.py
+++ b/solution.py
@@ -9,8 +9,12 @@
 BLK = 512
 TOK = 64
 HEADS = 8
-SEQ = 128
+PLANE = 4
+DEPTH = 32
 WIN = 5
+CHUNKS = 4
+CROWS = BLK // CHUNKS
+HALF = BLK // 2
 LOG2E = 1.4426950408889634
 SCALE = 1.0 / D**0.5
 BIG = 1e30
@@ -36,7 +40,7 @@
     q_hbm, do_hbm, o_hbm, k_hbm, v_hbm, lse_hbm, pairs_hbm,
     oq_ref, ok_ref, ov_ref,
     kv, qs, dos, do_own, o_own, lse, pairs, dls, dlr, accq, own_g, gsend, grecv, fin_q, fin_kv,
-    loc_sem, in_recv, in_send, kv_recv, kv_send, g_recv, g_send, out_recv, out_send,
+    loc_sem, in_recv, in_send, kvz_recv, kvz_send, kv_recv, kv_send, g_recv, g_send, out_recv, out_send,
 ):
     s = lax.axis_index("seq")
     h = lax.axis_index("head")
@@ -48,15 +52,33 @@
     for c in (c_do, c_o, c_lse, c_pairs):
         c.start()
 
+    z = s // PLANE
+    y = lax.rem(s, PLANE)
+
+    def in_plane(step):
+        return z * PLANE + lax.rem(y + step, PLANE)
+
+    up = lax.rem(s + PLANE, PLANE * DEPTH)
+    down = lax.rem(s + PLANE * (DEPTH - 1), PLANE * DEPTH)
+
+    above = (z + DEPTH - 1) // DEPTH
+    below = (2 * DEPTH - 2 - z) // DEPTH
     barrier = pltpu.get_barrier_semaphore()
     for j in range(1, HEADS):
         pl.semaphore_signal(barrier, inc=1, device_id=(s, lax.rem(h + j, HEADS)), device_id_type=MESH)
-    for j in range(1, WIN):
-        pl.semaphore_signal(barrier, inc=1, device_id=(lax.rem(s + j, SEQ), h), device_id_type=MESH)
-        pl.semaphore_signal(
-            barrier, inc=1, device_id=(lax.rem(s + SEQ - j, SEQ), h), device_id_type=MESH
-        )
-    pl.semaphore_wait(barrier, HEADS - 1 + 2 * (WIN - 1))
+    for d in range(1, PLANE):
+
+        @pl.when((d <= y) | (z > 0))
+        def _():
+            pl.semaphore_signal(
+                barrier, inc=1, device_id=(in_plane(PLANE - d), h), device_id_type=MESH
+            )
+
+    @pl.when(z > 0)
+    def _():
+        pl.semaphore_signal(barrier, inc=1, device_id=(down, h), device_id_type=MESH)
+
+    pl.semaphore_wait(barrier, HEADS - 1 + (PLANE - 1 - y) + above * y + below)
 
     my_rows = pl.ds(pl.multiple_of(h * TOK, TOK), TOK)
 
@@ -111,15 +133,48 @@
     pltpu.make_async_copy(dls.at[h], dlr.at[h], in_recv.at[3]).start()
 
     wait_bytes(kv.at[0], in_recv.at[0])
-    for d in (2, 4, 3, 1):
+
+    def kv_in_plane(d, slot, rows, half):
         pltpu.make_async_remote_copy(
-            src_ref=kv.at[0],
-            dst_ref=kv.at[d],
-            send_sem=kv_send,
-            recv_sem=kv_recv.at[d],
-            device_id=(lax.rem(s + d, SEQ), h),
+            src_ref=kv.at[slot, rows],
+            dst_ref=kv.at[d, rows],
+            send_sem=kv_send.at[2 * d + half],
+            recv_sem=kv_recv.at[2 * d + half],
+            device_id=(in_plane(d), h),
             device_id_type=MESH,
         ).start()
+
+    for half in range(2):
+
+        @pl.when(z < DEPTH - 1)
+        def _():
+            for i in range(half * CHUNKS // 2, (half + 1) * CHUNKS // 2):
+                rows = slice(i * CROWS, (i + 1) * CROWS)
+                pltpu.make_async_remote_copy(
+                    src_ref=kv.at[0, rows],
+                    dst_ref=kv.at[4, rows],
+                    send_sem=kvz_send.at[i],
+                    recv_sem=kvz_recv.at[i],
+                    device_id=(up, h),
+                    device_id_type=MESH,
+                ).start()
+
+        for d in (2, 3, 1):
+
+            @pl.when(y + d < PLANE)
+            def _():
+                kv_in_plane(d, 0, slice(half * HALF, (half + 1) * HALF), half)
+
+    @pl.when((z > 0) & (y > 0))
+    def _():
+        for i in range(CHUNKS):
+            rows = slice(i * CROWS, (i + 1) * CROWS)
+            wait_bytes(kv.at[4, rows], kvz_recv.at[i])
+            for d in (2, 3, 1):
+
+                @pl.when(y + d >= PLANE)
+                def _():
+                    kv_in_plane(d, 4, rows, 2 * i // CHUNKS)
 
     c_lse.wait()
     c_pairs.wait()
@@ -134,26 +189,44 @@
     delta = jnp.concatenate([dlr[2 * i] + dlr[2 * i + 1] for i in range(HEADS // 2)], axis=1)
     lse2 = lse[...] * LOG2E
 
-    def pair_step(pd, carry):
-        d = lax.rem(3 * pd, WIN)
-
-        @pl.when(pd > 0)
-        def _():
-            wait_bytes(kv.at[d], kv_recv.at[d])
+    def pair_step(t, carry):
+        late = t // 8
+        d = late * 4 + (1 - late) * lax.rem(t, 4)
+        half = late * lax.rem(t, 4) + (1 - late) * (t // 4)
+
+        @pl.when((z > 0) | (d <= y))
+        def _():
+            half_pair(d, half)
+
+        return carry
+
+    def half_pair(d, half):
+        rows = pl.ds(pl.multiple_of(half * HALF, HALF), HALF)
+
+        @pl.when((d > 0) & (d < 4))
+        def _():
+            wait_bytes(kv.at[d, rows], kv_recv.at[2 * d + half])
+
+        @pl.when((d == 4) & (y == 0))
+        def _():
+            for i in range(CHUNKS // 2):
+                wait_bytes(kv.at[4, 0:CROWS], kvz_recv.at[half * (CHUNKS // 2) + i])
 
         match = (pa == s) & (pc == s - d)
         code = jnp.max(jnp.where(match, pm + 1, 0), axis=1, keepdims=True)
         lo = jnp.where((code == 1) | (code == 2), -BLK, jnp.where(code == 3, 0, BLK))
         hi = jnp.where(code == 2, 1, BLK)
-        diff = lax.broadcasted_iota(jnp.int32, (BLK, BLK), 0) - lax.broadcasted_iota(
-            jnp.int32, (BLK, BLK), 1
+        diff = (
+            lax.broadcasted_iota(jnp.int32, (HALF, BLK), 0)
+            + half * HALF
+            - lax.broadcasted_iota(jnp.int32, (HALF, BLK), 1)
         )
         bias = jnp.where((diff > lo) & (diff < hi), 0.0, BIG).astype(F32)
-        k = kv[d, :, 0:D]
-        v = kv[d, :, D : 2 * D]
+        k = kv[d, rows, 0:D]
+        v = kv[d, rows, D : 2 * D]
         kt = k.T
-        gk = jnp.zeros((BLK, D), F32)
-        gv = jnp.zeros((BLK, D), F32)
+        gk = jnp.zeros((HALF, D), F32)
+        gv = jnp.zeros((HALF, D), F32)
         for g in range(2):
             c = slice(g * D, (g + 1) * D)
             q = qs[:, c]
@@ -164,57 +237,96 @@
             gk = gk + dot_nn(ds, q)
             accq[c, :] += dot_nn(kt, ds)
 
-        @pl.when(pd == 0)
-        def _():
-            own_g[:, 0:D] = gk
-            own_g[:, D : 2 * D] = gv
-
-        @pl.when(pd > 0)
-        def _():
-            gsend[d, :, 0:D] = gk.astype(BF16)
-            gsend[d, :, D : 2 * D] = gv.astype(BF16)
+        keep = (d == 0) | (d == 4)
+
+        @pl.when(keep)
+        def _():
+            own_g[d // 4, rows, 0:D] = gk
+            own_g[d // 4, rows, D : 2 * D] = gv
+
+        @pl.when(jnp.logical_not(keep))
+        def _():
+            gsend[d, rows, 0:D] = gk.astype(BF16)
+            gsend[d, rows, D : 2 * D] = gv.astype(BF16)
             pltpu.make_async_remote_copy(
-                src_ref=gsend.at[d],
-                dst_ref=grecv.at[d],
-                send_sem=g_send,
-                recv_sem=g_recv.at[d],
-                device_id=(lax.rem(s + SEQ - d, SEQ), h),
+                src_ref=gsend.at[d, rows],
+                dst_ref=grecv.at[d, rows],
+                send_sem=g_send.at[2 * d + half],
+                recv_sem=g_recv.at[2 * d + half],
+                device_id=(in_plane(PLANE - d), h),
                 device_id_type=MESH,
             ).start()
 
-        return carry
-
-    lax.fori_loop(0, WIN, pair_step, 0)
-
-    def gather(src, col, width, dst, n):
-        for j in PEER_ORDER:
-            p = lax.rem(h + j, HEADS)
+    lax.fori_loop(0, 2 * WIN, pair_step, 0)
+
+    def gather(src, col, width, dst, n, half):
+        for j in range(HEADS // 2):
+            p = half * (HEADS // 2) + lax.rem(h + j, HEADS // 2)
+
+            @pl.when(p != h)
+            def _():
+                pltpu.make_async_remote_copy(
+                    src_ref=src.at[cols(p, TOK), col],
+                    dst_ref=dst.at[:, cols(h, width)],
+                    send_sem=out_send.at[n],
+                    recv_sem=out_recv.at[n],
+                    device_id=(s, p),
+                    device_id_type=MESH,
+                ).start()
+
+            @pl.when(p == h)
+            def _():
+                pltpu.make_async_copy(
+                    src.at[my_rows, col], dst.at[:, cols(h, width)], out_recv.at[n]
+                ).start()
+
+    halves = (slice(0, HALF), slice(HALF, BLK))
+
+    def to_plane_before(i):
+        @pl.when(z > 0)
+        def _():
+            for d in (1, 2, 3):
+
+                @pl.when(y + d >= PLANE)
+                def _():
+                    wait_bytes(grecv.at[d, halves[i]], g_recv.at[2 * d + i])
+                    own_g[1, halves[i]] += grecv[d, halves[i]].astype(F32)
+
+            gsend[0, halves[i]] = own_g[1, halves[i]].astype(BF16)
             pltpu.make_async_remote_copy(
-                src_ref=src.at[cols(p, TOK), col],
-                dst_ref=dst.at[:, cols(h, width)],
-                send_sem=out_send.at[n],
-                recv_sem=out_recv.at[n],
-                device_id=(s, p),
+                src_ref=gsend.at[0, halves[i]],
+                dst_ref=grecv.at[0, halves[i]],
+                send_sem=g_send.at[i],
+                recv_sem=g_recv.at[i],
+                device_id=(down, h),
                 device_id_type=MESH,
             ).start()
-        pltpu.make_async_copy(
-            src.at[my_rows, col], dst.at[:, cols(h, width)], out_recv.at[n]
-        ).start()
-
+
+    to_plane_before(0)
     for g in range(2):
         c = slice(g * D, (g + 1) * D)
         fin_q[:, c] = (accq[c, :] * SCALE).T.astype(BF16)
-    gather(fin_q, slice(0, 2 * D), 2 * D, oq_ref, 0)
-
-    for d in range(1, WIN):
-        wait_bytes(grecv.at[d], g_recv.at[d])
-    tot = own_g[...]
-    for d in range(1, WIN):
-        tot = tot + grecv[d].astype(F32)
-    fin_kv[:, 0:D] = (tot[:, 0:D] * SCALE).astype(BF16)
-    fin_kv[:, D : 2 * D] = tot[:, D : 2 * D].astype(BF16)
-    gather(fin_kv, slice(0, D), D, ok_ref, 1)
-    gather(fin_kv, slice(D, 2 * D), D, ov_ref, 2)
+    for half in range(2):
+        gather(fin_q, slice(0, 2 * D), 2 * D, oq_ref, 0, half)
+    to_plane_before(1)
+
+    for i in range(2):
+        for d in (1, 2, 3):
+
+            @pl.when(y + d < PLANE)
+            def _():
+                wait_bytes(grecv.at[d, halves[i]], g_recv.at[2 * d + i])
+                own_g[0, halves[i]] += grecv[d, halves[i]].astype(F32)
+
+        @pl.when(z < DEPTH - 1)
+        def _():
+            wait_bytes(grecv.at[0, halves[i]], g_recv.at[i])
+            own_g[0, halves[i]] += grecv[0, halves[i]].astype(F32)
+
+        fin_kv[halves[i], 0:D] = (own_g[0, halves[i], 0:D] * SCALE).astype(BF16)
+        fin_kv[halves[i], D : 2 * D] = own_g[0, halves[i], D : 2 * D].astype(BF16)
+        gather(fin_kv, slice(0, D), D, ok_ref, 1, i)
+        gather(fin_kv, slice(D, 2 * D), D, ov_ref, 2, i)
 
     most = (HEADS - 1) * TOK
     wait_bytes(kv.at[0, 0:most, 0:D], in_send.at[0])
@@ -222,8 +334,28 @@
     wait_bytes(qs.at[0:most], in_send.at[2])
     wait_bytes(qs.at[0:most], in_send.at[3])
     wait_bytes(dlr.at[0 : HEADS - 1], in_send.at[4])
-    wait_bytes(kv.at[1:WIN], kv_send)
-    wait_bytes(gsend.at[1:WIN], g_send)
+
+    @pl.when(z < DEPTH - 1)
+    def _():
+        for i in range(CHUNKS):
+            wait_bytes(kv.at[0, 0:CROWS], kvz_send.at[i])
+
+    for i in range(2):
+
+        @pl.when(z > 0)
+        def _():
+            wait_bytes(gsend.at[0, halves[i]], g_send.at[i])
+
+        for d in range(1, PLANE):
+
+            @pl.when((y + d < PLANE) | (z > 0))
+            def _():
+                wait_bytes(kv.at[d, halves[i]], kv_send.at[2 * d + i])
+
+            @pl.when((d <= y) | (z > 0))
+            def _():
+                wait_bytes(gsend.at[d, halves[i]], g_send.at[2 * d + i])
+
     wait_bytes(fin_q.at[0:most], out_send.at[0])
     wait_bytes(fin_kv.at[0:most, 0:D], out_send.at[1])
     wait_bytes(fin_kv.at[0:most, 0:D], out_send.at[2])
@@ -232,15 +364,33 @@
     wait_bytes(ov_ref, out_recv.at[2])
 
 
+def hand_on(q_ref, k_ref, v_ref, oq_ref, ok_ref, ov_ref, q_buf, k_buf, v_buf, sem_in, sem_out):
+    buffers = ((q_ref, q_buf, oq_ref), (k_ref, k_buf, ok_ref), (v_ref, v_buf, ov_ref))
+    arrive = [
+        pltpu.make_async_copy(src, buf, sem_in.at[n]) for n, (src, buf, dst) in enumerate(buffers)
+    ]
+    leave = [
+        pltpu.make_async_copy(buf, dst, sem_out.at[n]) for n, (src, buf, dst) in enumerate(buffers)
+    ]
+    for c in arrive:
+        c.start()
+    for a, b in zip(arrive, leave):
+        a.wait()
+        b.start()
+    for c in leave:
+        c.wait()
+
+
 def shards(queries, output_gradient, outputs, key_vectors, values, logsum, pair_list):
     any_spec = pl.BlockSpec(memory_space=pl.ANY)
-    return pl.pallas_call(
+    out_shape = (
+        jax.ShapeDtypeStruct((TOK, 2 * D * HEADS), BF16),
+        jax.ShapeDtypeStruct((TOK, D * HEADS), BF16),
+        jax.ShapeDtypeStruct((TOK, D * HEADS), BF16),
+    )
+    grads = pl.pallas_call(
         kernel,
-        out_shape=(
-            jax.ShapeDtypeStruct((TOK, 2 * D * HEADS), BF16),
-            jax.ShapeDtypeStruct((TOK, D * HEADS), BF16),
-            jax.ShapeDtypeStruct((TOK, D * HEADS), BF16),
-        ),
+        out_shape=out_shape,
         in_specs=[any_spec] * 7,
         out_specs=(any_spec,) * 3,
         scratch_shapes=[
@@ -254,18 +404,20 @@
             pltpu.VMEM((HEADS, 8, D), F32),
             pltpu.VMEM((HEADS, 8, D), F32),
             pltpu.VMEM((2 * D, BLK), F32),
-            pltpu.VMEM((BLK, 2 * D), F32),
-            pltpu.VMEM((WIN, BLK, 2 * D), BF16),
-            pltpu.VMEM((WIN, BLK, 2 * D), BF16),
+            pltpu.VMEM((2, BLK, 2 * D), F32),
+            pltpu.VMEM((PLANE, BLK, 2 * D), BF16),
+            pltpu.VMEM((PLANE, BLK, 2 * D), BF16),
             pltpu.VMEM((BLK, 2 * D), BF16),
             pltpu.VMEM((BLK, 2 * D), BF16),
             pltpu.SemaphoreType.DMA((4,)),
             pltpu.SemaphoreType.DMA((4,)),
             pltpu.SemaphoreType.DMA((5,)),
-            pltpu.SemaphoreType.DMA((WIN,)),
-            pltpu.SemaphoreType.DMA,
-            pltpu.SemaphoreType.DMA((WIN,)),
-            pltpu.SemaphoreType.DMA,
+            pltpu.SemaphoreType.DMA((CHUNKS,)),
+            pltpu.SemaphoreType.DMA((CHUNKS,)),
+            pltpu.SemaphoreType.DMA((2 * PLANE,)),
+            pltpu.SemaphoreType.DMA((2 * PLANE,)),
+            pltpu.SemaphoreType.DMA((2 * PLANE,)),
+            pltpu.SemaphoreType.DMA((2 * PLANE,)),
             pltpu.SemaphoreType.DMA((3,)),
             pltpu.SemaphoreType.DMA((3,)),
         ],
@@ -280,6 +432,15 @@
     )(
         queries, output_gradient, outputs, key_vectors, values, logsum, jnp.transpose(pair_list)
     )
+    return pl.pallas_call(
+        hand_on,
+        out_shape=out_shape,
+        in_specs=[any_spec] * 3,
+        out_specs=(any_spec,) * 3,
+        scratch_shapes=[pltpu.VMEM(o.shape, o.dtype) for o in out_shape]
+        + [pltpu.SemaphoreType.DMA((3,)), pltpu.SemaphoreType.DMA((3,))],
+        compiler_params=pltpu.CompilerParams(vmem_limit_bytes=60 * 2**20),
+    )(*grads)
 
 
 def solution(mesh):

time: 81 us -> 55.3 us (0.68)
  the two profiles are of different devices: /device:TPU:17 before, /device:TPU:877 now
where the time goes in v2:
time: 55.3 us; the launch traced here: 55.2 us
  Pallas kernels  54.5 us (99%)
  between operations  0.64 us (1%)
    pallas_call x1, Pallas kernels, shards(): pl.pallas_call(kernel, out_shape=out_shape, in_specs=[any_spec] * 7, out_...  52.7 us
    pallas_call x1, Pallas kernels, shards(): pl.pallas_call(hand_on, out_shape=out_shape, in_specs=[any_spec] * 3, out...  1.79 us

profile of v2, /device:TPU:877, one launch (start us, length us, event | category | flops | bytes accessed | tf_op | source)
XLA Modules:
  0.0 55.2 jit_solution(3810374162666521577)
XLA Ops:
  0.6 52.7 %shard_map.94 = (bf16[64,2048]{1,0:T(8,128)(2,1)}, bf16[64,1024]{1,0:T(8,128)(2,1)}, bf16[64,1024]{1,0:T(8,128)(2,1)}) custom-call(bf16[64,2048]{1,0:T(8,128)(2,1)} %q_hbm.1, bf16[64,2048]{1,0:T(8,128)(2,1)} %do_hbm.1, bf16[64,2048]{1,0:T(8,128)(2,1)} %o_hbm.1, bf16[64,1024]{1,0:T(8,128)(2,1)} %k_hbm.1, bf16[64,1024]{1,0:T(8,128)(2,1)} %v_hbm.1, ...), custom_call_target="tpu_custom_call" | custom-call | flops 3355443200 | bytes 1572864 | tf_op jit(solution)/shard_map/pallas_call | solution.py:391
  53.4 1.8 %shard_map.95 = (bf16[64,2048]{1,0:T(8,128)(2,1)}, bf16[64,1024]{1,0:T(8,128)(2,1)}, bf16[64,1024]{1,0:T(8,128)(2,1)}) custom-call(bf16[64,2048]{1,0:T(8,128)(2,1)} %get-tuple-element.6.q_ref, bf16[64,1024]{1,0:T(8,128)(2,1)} %get-tuple-element.7.k_ref, bf16[64,1024]{1,0:T(8,128)(2,1)} %get-tuple-element.8.v_ref), custom_call_target="tpu_custom_call" | custom-call | tf_op jit(solution)/shard_map/pallas_call | solution.py:435

commit v3 on v2

--- a/solution.py
+++ b/solution.py
@@ -189,6 +189,17 @@
     delta = jnp.concatenate([dlr[2 * i] + dlr[2 * i + 1] for i in range(HEADS // 2)], axis=1)
     lse2 = lse[...] * LOG2E
 
+    def send_back(d, half):
+        rows = pl.ds(pl.multiple_of(half * HALF, HALF), HALF)
+        pltpu.make_async_remote_copy(
+            src_ref=gsend.at[d, rows],
+            dst_ref=grecv.at[d, rows],
+            send_sem=g_send.at[2 * d + half],
+            recv_sem=g_recv.at[2 * d + half],
+            device_id=(in_plane(PLANE - d), h),
+            device_id_type=MESH,
+        ).start()
+
     def pair_step(t, carry):
         late = t // 8
         d = late * 4 + (1 - late) * lax.rem(t, 4)
@@ -248,16 +259,20 @@
         def _():
             gsend[d, rows, 0:D] = gk.astype(BF16)
             gsend[d, rows, D : 2 * D] = gv.astype(BF16)
-            pltpu.make_async_remote_copy(
-                src_ref=gsend.at[d, rows],
-                dst_ref=grecv.at[d, rows],
-                send_sem=g_send.at[2 * d + half],
-                recv_sem=g_recv.at[2 * d + half],
-                device_id=(in_plane(PLANE - d), h),
-                device_id_type=MESH,
-            ).start()
-
-    lax.fori_loop(0, 2 * WIN, pair_step, 0)
+
+            @pl.when(d > y)
+            def _():
+                send_back(d, half)
+
+    lax.fori_loop(0, 2 * PLANE, pair_step, 0)
+    for half in range(2):
+        for d in range(1, PLANE):
+
+            @pl.when(d <= y)
+            def _():
+                send_back(d, half)
+
+    lax.fori_loop(2 * PLANE, 2 * WIN, pair_step, 0)
 
     def gather(src, col, width, dst, n, half):
         for j in range(HEADS // 2):

time: 55.3 us -> 52.8 us (0.955)
  the two profiles are of different devices: /device:TPU:877 before, /device:TPU:749 now
where the time goes in v3:
time: 52.8 us; the launch traced here: 52.6 us
  Pallas kernels  52 us (98%)
  between operations  0.64 us (1%)
    pallas_call x1, Pallas kernels, shards(): pl.pallas_call(kernel, out_shape=out_shape, in_specs=[any_spec] * 7, out_...  50.2 us
    pallas_call x1, Pallas kernels, shards(): pl.pallas_call(hand_on, out_shape=out_shape, in_specs=[any_spec] * 3, out...  1.79 us

profile of v3, /device:TPU:749, one launch (start us, length us, event | category | flops | bytes accessed | tf_op | source)
XLA Modules:
  0.0 52.6 jit_solution(2196016478846796171)
XLA Ops:
  0.6 50.2 %shard_map.94 = (bf16[64,2048]{1,0:T(8,128)(2,1)}, bf16[64,1024]{1,0:T(8,128)(2,1)}, bf16[64,1024]{1,0:T(8,128)(2,1)}) custom-call(bf16[64,2048]{1,0:T(8,128)(2,1)} %q_hbm.1, bf16[64,2048]{1,0:T(8,128)(2,1)} %do_hbm.1, bf16[64,2048]{1,0:T(8,128)(2,1)} %o_hbm.1, bf16[64,1024]{1,0:T(8,128)(2,1)} %k_hbm.1, bf16[64,1024]{1,0:T(8,128)(2,1)} %v_hbm.1, ...), custom_call_target="tpu_custom_call" | custom-call | flops 3355443200 | bytes 1572864 | tf_op jit(solution)/shard_map/pallas_call | solution.py:406
  50.8 1.8 %shard_map.95 = (bf16[64,2048]{1,0:T(8,128)(2,1)}, bf16[64,1024]{1,0:T(8,128)(2,1)}, bf16[64,1024]{1,0:T(8,128)(2,1)}) custom-call(bf16[64,2048]{1,0:T(8,128)(2,1)} %get-tuple-element.6.q_ref, bf16[64,1024]{1,0:T(8,128)(2,1)} %get-tuple-element.7.k_ref, bf16[64,1024]{1,0:T(8,128)(2,1)} %get-tuple-element.8.v_ref), custom_call_target="tpu_custom_call" | custom-call | tf_op jit(solution)/shard_map/pallas_call | solution.py:450

commit v4 on v3

--- a/solution.py
+++ b/solution.py
@@ -201,9 +201,12 @@
         ).start()
 
     def pair_step(t, carry):
-        late = t // 8
-        d = late * 4 + (1 - late) * lax.rem(t, 4)
-        half = late * lax.rem(t, 4) + (1 - late) * (t // 4)
+        first_row = 1 - (y + 2) // 3
+        u = t + first_row * (2 * ((t + 6) // 8) - 8 * (t // 8))
+        a = (u + 8) // 10
+        b = (u + 6) // 10
+        d = 4 * (a - b) + b * (1 + lax.rem(12 + first_row - u, 3))
+        half = (1 - a) * u + (a - b) * (u - 2) + b * ((u + 2) // 3 - 2)
 
         @pl.when((z > 0) | (d <= y))
         def _():
@@ -260,19 +263,18 @@
             gsend[d, rows, 0:D] = gk.astype(BF16)
             gsend[d, rows, D : 2 * D] = gv.astype(BF16)
 
-            @pl.when(d > y)
+            @pl.when((d > y) | (z == 0))
             def _():
                 send_back(d, half)
 
-    lax.fori_loop(0, 2 * PLANE, pair_step, 0)
+    lax.fori_loop(0, 2 * WIN, pair_step, 0)
     for half in range(2):
         for d in range(1, PLANE):
 
-            @pl.when(d <= y)
+            @pl.when((d <= y) & (z > 0))
             def _():
                 send_back(d, half)
 
-    lax.fori_loop(2 * PLANE, 2 * WIN, pair_step, 0)
 
     def gather(src, col, width, dst, n, half):
         for j in range(HEADS // 2):

time: 52.8 us -> 52.6 us (level)
  the two profiles are of different devices: /device:TPU:749 before, /device:TPU:119 now
where the time goes in v4:
time: 52.6 us; the launch traced here: 52.4 us
  Pallas kernels  51.8 us (98%)
  between operations  0.64 us (1%)
    pallas_call x1, Pallas kernels, shards(): pl.pallas_call(kernel, out_shape=out_shape, in_specs=[any_spec] * 7, out_...  50 us
    pallas_call x1, Pallas kernels, shards(): pl.pallas_call(hand_on, out_shape=out_shape, in_specs=[any_spec] * 3, out...  1.79 us

profile of v4, /device:TPU:119, one launch (start us, length us, event | category | flops | bytes accessed | tf_op | source)
XLA Modules:
  0.0 52.4 jit_solution(17202438579782879285)
XLA Ops:
  0.6 50.0 %shard_map.94 = (bf16[64,2048]{1,0:T(8,128)(2,1)}, bf16[64,1024]{1,0:T(8,128)(2,1)}, bf16[64,1024]{1,0:T(8,128)(2,1)}) custom-call(bf16[64,2048]{1,0:T(8,128)(2,1)} %q_hbm.1, bf16[64,2048]{1,0:T(8,128)(2,1)} %do_hbm.1, bf16[64,2048]{1,0:T(8,128)(2,1)} %o_hbm.1, bf16[64,1024]{1,0:T(8,128)(2,1)} %k_hbm.1, bf16[64,1024]{1,0:T(8,128)(2,1)} %v_hbm.1, ...), custom_call_target="tpu_custom_call" | custom-call | flops 3355443200 | bytes 1572864 | tf_op jit(solution)/shard_map/pallas_call | solution.py:408
  50.7 1.8 %shard_map.95 = (bf16[64,2048]{1,0:T(8,128)(2,1)}, bf16[64,1024]{1,0:T(8,128)(2,1)}, bf16[64,1024]{1,0:T(8,128)(2,1)}) custom-call(bf16[64,2048]{1,0:T(8,128)(2,1)} %get-tuple-element.6.q_ref, bf16[64,1024]{1,0:T(8,128)(2,1)} %get-tuple-element.7.k_ref, bf16[64,1024]{1,0:T(8,128)(2,1)} %get-tuple-element.8.v_ref), custom_call_target="tpu_custom_call" | custom-call | tf_op jit(solution)/shard_map/pallas_call | solution.py:452

commit v5 on v4

--- a/solution.py
+++ b/solution.py
@@ -276,9 +276,9 @@
                 send_back(d, half)
 
 
-    def gather(src, col, width, dst, n, half):
-        for j in range(HEADS // 2):
-            p = half * (HEADS // 2) + lax.rem(h + j, HEADS // 2)
+    def gather(src, col, width, dst, n, first, count):
+        for j in range(count):
+            p = first + lax.rem(h + j, count)
 
             @pl.when(p != h)
             def _():
@@ -298,6 +298,8 @@
                 ).start()
 
     halves = (slice(0, HALF), slice(HALF, BLK))
+    middle = HALF + HALF // 2
+    pieces = (((0, HALF, 0),), ((HALF, middle, 1), (middle, BLK, 2 * PLANE)))
 
     def to_plane_before(i):
         @pl.when(z > 0)
@@ -309,22 +311,24 @@
                     wait_bytes(grecv.at[d, halves[i]], g_recv.at[2 * d + i])
                     own_g[1, halves[i]] += grecv[d, halves[i]].astype(F32)
 
-            gsend[0, halves[i]] = own_g[1, halves[i]].astype(BF16)
-            pltpu.make_async_remote_copy(
-                src_ref=gsend.at[0, halves[i]],
-                dst_ref=grecv.at[0, halves[i]],
-                send_sem=g_send.at[i],
-                recv_sem=g_recv.at[i],
-                device_id=(down, h),
-                device_id_type=MESH,
-            ).start()
+            for low_row, end, n in pieces[i]:
+                rows = slice(low_row, end)
+                gsend[0, rows] = own_g[1, rows].astype(BF16)
+                pltpu.make_async_remote_copy(
+                    src_ref=gsend.at[0, rows],
+                    dst_ref=grecv.at[0, rows],
+                    send_sem=g_send.at[n],
+                    recv_sem=g_recv.at[n],
+                    device_id=(down, h),
+                    device_id_type=MESH,
+                ).start()
 
     to_plane_before(0)
     for g in range(2):
         c = slice(g * D, (g + 1) * D)
         fin_q[:, c] = (accq[c, :] * SCALE).T.astype(BF16)
     for half in range(2):
-        gather(fin_q, slice(0, 2 * D), 2 * D, oq_ref, 0, half)
+        gather(fin_q, slice(0, 2 * D), 2 * D, oq_ref, 0, half * (HEADS // 2), HEADS // 2)
     to_plane_before(1)
 
     for i in range(2):
@@ -335,15 +339,19 @@
                 wait_bytes(grecv.at[d, halves[i]], g_recv.at[2 * d + i])
                 own_g[0, halves[i]] += grecv[d, halves[i]].astype(F32)
 
-        @pl.when(z < DEPTH - 1)
-        def _():
-            wait_bytes(grecv.at[0, halves[i]], g_recv.at[i])
-            own_g[0, halves[i]] += grecv[0, halves[i]].astype(F32)
-
-        fin_kv[halves[i], 0:D] = (own_g[0, halves[i], 0:D] * SCALE).astype(BF16)
-        fin_kv[halves[i], D : 2 * D] = own_g[0, halves[i], D : 2 * D].astype(BF16)
-        gather(fin_kv, slice(0, D), D, ok_ref, 1, i)
-        gather(fin_kv, slice(D, 2 * D), D, ov_ref, 2, i)
+        for low_row, end, n in pieces[i]:
+            rows = slice(low_row, end)
+
+            @pl.when(z < DEPTH - 1)
+            def _():
+                wait_bytes(grecv.at[0, rows], g_recv.at[n])
+                own_g[0, rows] += grecv[0, rows].astype(F32)
+
+            fin_kv[rows, 0:D] = (own_g[0, rows, 0:D] * SCALE).astype(BF16)
+            fin_kv[rows, D : 2 * D] = own_g[0, rows, D : 2 * D].astype(BF16)
+            peers = (low_row // TOK, (end - low_row) // TOK)
+            gather(fin_kv, slice(0, D), D, ok_ref, 1, *peers)
+            gather(fin_kv, slice(D, 2 * D), D, ov_ref, 2, *peers)
 
     most = (HEADS - 1) * TOK
     wait_bytes(kv.at[0, 0:most, 0:D], in_send.at[0])
@@ -361,7 +369,8 @@
 
         @pl.when(z > 0)
         def _():
-            wait_bytes(gsend.at[0, halves[i]], g_send.at[i])
+            for low_row, end, n in pieces[i]:
+                wait_bytes(gsend.at[0, low_row:end], g_send.at[n])
 
         for d in range(1, PLANE):
 
@@ -433,8 +442,8 @@
             pltpu.SemaphoreType.DMA((CHUNKS,)),
             pltpu.SemaphoreType.DMA((2 * PLANE,)),
             pltpu.SemaphoreType.DMA((2 * PLANE,)),
-            pltpu.SemaphoreType.DMA((2 * PLANE,)),
-            pltpu.SemaphoreType.DMA((2 * PLANE,)),
+            pltpu.SemaphoreType.DMA((2 * PLANE + 1,)),
+            pltpu.SemaphoreType.DMA((2 * PLANE + 1,)),
             pltpu.SemaphoreType.DMA((3,)),
             pltpu.SemaphoreType.DMA((3,)),
         ],

time: 52.6 us -> 52.6 us (level)
  no operation moved by 1% of the time
where the time goes in v5:
time: 52.6 us; the launch traced here: 52.4 us
  Pallas kernels  51.8 us (98%)
  between operations  0.64 us (1%)
    pallas_call x1, Pallas kernels, shards(): pl.pallas_call(kernel, out_shape=out_shape, in_specs=[any_spec] * 7, out_...  50 us
    pallas_call x1, Pallas kernels, shards(): pl.pallas_call(hand_on, out_shape=out_shape, in_specs=[any_spec] * 3, out...  1.79 us

profile of v5, /device:TPU:119, one launch (start us, length us, event | category | flops | bytes accessed | tf_op | source)
XLA Modules:
  0.0 52.4 jit_solution(10506760951858380930)
XLA Ops:
  0.6 50.0 %shard_map.94 = (bf16[64,2048]{1,0:T(8,128)(2,1)}, bf16[64,1024]{1,0:T(8,128)(2,1)}, bf16[64,1024]{1,0:T(8,128)(2,1)}) custom-call(bf16[64,2048]{1,0:T(8,128)(2,1)} %q_hbm.1, bf16[64,2048]{1,0:T(8,128)(2,1)} %do_hbm.1, bf16[64,2048]{1,0:T(8,128)(2,1)} %o_hbm.1, bf16[64,1024]{1,0:T(8,128)(2,1)} %k_hbm.1, bf16[64,1024]{1,0:T(8,128)(2,1)} %v_hbm.1, ...), custom_call_target="tpu_custom_call" | custom-call | flops 3355443200 | bytes 1572864 | tf_op jit(solution)/shard_map/pallas_call | solution.py:417
  50.7 1.8 %shard_map.95 = (bf16[64,2048]{1,0:T(8,128)(2,1)}, bf16[64,1024]{1,0:T(8,128)(2,1)}, bf16[64,1024]{1,0:T(8,128)(2,1)}) custom-call(bf16[64,2048]{1,0:T(8,128)(2,1)} %get-tuple-element.6.q_ref, bf16[64,1024]{1,0:T(8,128)(2,1)} %get-tuple-element.7.k_ref, bf16[64,1024]{1,0:T(8,128)(2,1)} %get-tuple-element.8.v_ref), custom_call_target="tpu_custom_call" | custom-call | tf_op jit(solution)/shard_map/pallas_call | solution.py:461
